TPU v7x, 1024 devices: a whole 8x8x8 slice. The times are simulated.
1024 devices in a mesh: dp: 64 (over x, z), expert: 16 (over y, core).
Axes of the slice: x: 8, y: 8, z: 8, core: 2. Of those that a mesh axis runs over, the one named last changes fastest.
Arguments:
- d_out: bfloat16 [131072, 5120], P(('dp', 'expert')), may hold values from -6 to 6
- routes: int32 [131072, 1], P(('dp', 'expert')), may hold values from 0 to 15; in each aligned block of 128 rows (0 to 127, 128 to 255, ...) at most 10 rows name the same one
- gates: bfloat16 [131072, 1], P(('dp', 'expert')), may hold values from 0.01 to 1, as said below
- slot_hidden: bfloat16 [64, 16, 16, 10, 768], P('dp', None, 'expert'), may hold values from -0.59765625 to 0.59765625
- w_down: bfloat16 [16, 768, 5120], P('expert'), may hold values from -0.078125 to 0.078125
- balance_coef: float32 [], replicated, may hold values from 0.5 to 2
Outputs:
- d_probs: float32 [131072, 16], P(('dp', 'expert'))
- d_hidden: bfloat16 [64, 16, 16, 10, 768], P('dp', None, 'expert')
Inputs may be any that keep to these rules, and one draw needn't show every extreme that they name: `routes`: within each aligned block of 128 rows (the rows of one device) no expert is named by more than 10 pairs, a bound that some block reaches. `gates`: positive gate weights.
All inputs are finite; a program needn't handle non-finite values.
Results may differ from a plain program's by a relative error of at most 0.007.
Values may be sent and summed in bfloat16 or wider, within the bound.
No kernel may reach another device: no remote copies, remote signals or barrier semaphores. Data moves between devices by JAX's collectives and lax.ppermute only.
A program may use at most 64 MiB of HBM per device.

v0:
```python
import functools

import jax
import jax.numpy as jnp
from jax import lax
from jax.experimental import pallas as pl
from jax.experimental.pallas import tpu as pltpu
from jax.sharding import PartitionSpec as P

F32 = jnp.float32
BF16 = jnp.bfloat16
SUB = 8


RING = 8


def iota(shape, axis):
    return lax.broadcasted_iota(jnp.int32, shape, axis)


def interleave(tail_ref, blocks, start, late):
    tiles = tail_ref.shape[0]
    for k in range(late.shape[1] // 128):
        b, tile = divmod(start + k, tiles)
        tail_ref[tile, pl.ds(b, late.shape[0], stride=blocks), :] = late[:, k * 128 : (k + 1) * 128]


def pack_kernel(
    blocks, routes_any, gates_any, rows_any, send_ref, rank_ref, mass_ref, routes_ref, gates_ref, rows_ref, tail_ref, sems
):
    copies = [
        pltpu.make_async_copy(routes_any, routes_ref, sems.at[0]),
        pltpu.make_async_copy(gates_any, gates_ref, sems.at[1]),
        pltpu.make_async_copy(rows_any, rows_ref, sems.at[2]),
    ]
    for copy in copies:
        copy.start()
    tokens, width = rows_ref.shape
    out_rows = send_ref.shape[0]
    experts = out_rows // SUB
    part = width // blocks
    copies[0].wait()
    copies[1].wait()
    routes = routes_ref[...]
    gates = gates_ref[...].astype(F32)
    onehot = (iota((experts, tokens), 0) == routes).astype(F32)
    earlier = (iota((tokens, tokens), 0) < iota((tokens, tokens), 1)).astype(BF16)
    before = jnp.dot(onehot.astype(BF16), earlier, preferred_element_type=F32)
    rank = jnp.sum(before * onehot, axis=0, keepdims=True).astype(jnp.int32)
    rank_ref[...] = rank
    mass = jnp.sum(onehot * gates, axis=1, keepdims=True)
    lane = iota((SUB, mass_ref.shape[1]), 1)
    total = jnp.zeros(mass_ref.shape, F32)
    for half in range(experts // SUB):
        total += jnp.where(lane == 2 + half, mass[half * SUB : (half + 1) * SUB], 0.0)
    mass_ref[...] = total
    late_rows = out_rows // blocks
    row = iota((out_rows + late_rows, tokens), 0)
    late = out_rows + routes * (SUB // blocks) + (rank - SUB)
    place = jnp.where(rank < SUB, routes * SUB + rank, late)
    pick = jnp.where(row == place, gates, 0.0).astype(BF16)
    copies[2].wait()
    packed = jnp.dot(pick, rows_ref[...], preferred_element_type=F32)
    send_ref[:, :width] = packed[:out_rows].astype(BF16)
    interleave(tail_ref, blocks, 0, packed[out_rows:])
    for k in range(tail_ref.shape[0]):
        send_ref[:, width + k * 128 : width + (k + 1) * 128] = tail_ref[k].astype(BF16)


def slot_order(groups, slots, rows, axis):
    count = groups * slots
    line = (count, 1) if axis == 0 else (1, count)
    r = iota(line, axis)
    late = slots - SUB
    slot = jnp.where(r < rows, r % SUB, SUB + (r - rows) % late)
    source = jnp.where(r < rows, r // SUB, (r - rows) // late)
    return (iota((count, count), 1 - axis) == slot * groups + source).astype(BF16)


def expert_kernel(blocks, slots, hid_ref, w_any, y_ref, w_ref, tail_ref, sems):
    rows = y_ref.shape[0]
    groups = rows // SUB
    width = w_ref.shape[1]
    part = width // blocks
    half = part // 2
    cuts = [slice(at, at + half) for at in range(0, width, half)]
    copies = [
        pltpu.make_async_copy(w_any.at[:, cut], w_ref.at[:, cut], sems.at[i]) for i, cut in enumerate(cuts)
    ]
    for copy in copies:
        copy.start()
    order = slot_order(groups, slots, rows, 0)
    hid = jnp.dot(order, hid_ref[...], preferred_element_type=F32).astype(BF16)
    for i, cut in enumerate(cuts):
        copies[i].wait()
        y = jnp.dot(hid, w_ref[:, cut], preferred_element_type=F32)
        y_ref[:, cut] = y[:rows].astype(BF16)
        interleave(tail_ref, blocks, i * half // 128, y[rows:])
    for k in range(tail_ref.shape[0]):
        y_ref[:, width + k * 128 : width + (k + 1) * 128] = tail_ref[k].astype(BF16)


def score_kernel(width, recv_ref, y_ref, mass_ref, ret_ref):
    rows = recv_ref.shape[0]
    groups = rows // SUB
    main = jnp.zeros((rows, 128), F32)
    rest = jnp.zeros((rows, 128), F32)
    for lane in range(0, recv_ref.shape[1], 128):
        cut = slice(lane, lane + 128)
        term = recv_ref[:, cut].astype(F32) * y_ref[:, cut].astype(F32)
        if lane < width:
            main += term
        else:
            rest += term
    lane = iota(ret_ref.shape, 1)
    ret = jnp.where(lane == 0, jnp.sum(main, axis=1, keepdims=True), 0.0)
    ret += jnp.where(lane == 1, jnp.sum(rest, axis=1, keepdims=True), 0.0)
    mass = jnp.broadcast_to(mass_ref[...][None], (groups, SUB, mass_ref.shape[1]))
    ret_ref[...] = ret + mass.reshape(ret_ref.shape)


def hidden_kernel(blocks, slots, recv_ref, w_ref, after_any, dhid_ref, x_ref):
    del after_any
    rows = recv_ref.shape[0]
    width = x_ref.shape[1]
    part = width // blocks
    late_rows = rows // blocks

    @pl.when(pl.program_id(0) == 0)
    def _():
        x_ref[:rows, :] = recv_ref[:, :width]
        r = iota((late_rows, rows), 1)
        i = iota((late_rows, rows), 0)
        for b in range(blocks):
            take = (r == i * blocks + b).astype(BF16)
            late = jnp.dot(take, recv_ref[:, width:], preferred_element_type=F32)
            x_ref[rows:, b * part : (b + 1) * part] = late.astype(BF16)

    proj = lax.dot_general(
        x_ref[...], w_ref[...], (((1,), (1,)), ((), ())), preferred_element_type=F32
    )
    order = slot_order(rows // SUB, slots, rows, 1)
    dhid_ref[...] = jnp.dot(order, proj.astype(BF16), preferred_element_type=F32).astype(BF16)


def probs_kernel(blocks, scale, coef_ref, routes_ref, gates_ref, rank_ref, back_ref, out_ref):
    experts, tokens = out_ref.shape
    rows = back_ref.shape[0]
    routes = routes_ref[...]
    rank = rank_ref[...]
    gates = gates_ref[...].astype(F32)
    back = back_ref[...]
    row = iota((rows, tokens), 0)
    first = jnp.where(rank < SUB, routes * SUB + rank, -1)
    late = jnp.where(rank >= SUB, routes * (SUB // blocks) + (rank - SUB), -1)
    hits = jnp.where(row == first, back[:, 0:1], 0.0)
    hits += jnp.where(row // blocks == late, back[:, 1:2], 0.0)
    score = jnp.sum(hits, axis=0, keepdims=True) / gates
    mass = jnp.sum(back.reshape(rows // SUB, SUB, back.shape[1]), axis=0)
    coef = coef_ref[0, 0] * scale
    for half in range(experts // SUB):
        expert = iota((SUB, tokens), 0) + half * SUB
        load = mass[:, 2 + half : 3 + half] * coef
        out_ref[half * SUB : (half + 1) * SUB, :] = load + jnp.where(expert == routes, score, 0.0)


def on_device(d_out, routes, gates, slot_hidden, w_down, balance_coef):
    tokens, width = d_out.shape
    groups = lax.axis_size("expert")
    dp = lax.axis_size("dp")
    experts = groups * w_down.shape[0]
    slots, units = slot_hidden.shape[3:]
    blocks = SUB // (slots - SUB)
    part = width // blocks
    out_rows = experts * SUB
    routes_row = routes.reshape(1, tokens)
    gates_row = gates.reshape(1, tokens)
    vmem = pltpu.CompilerParams(vmem_limit_bytes=32 * 1024 * 1024)
    streams = pltpu.CompilerParams(vmem_limit_bytes=50 * 1024 * 1024)
    anywhere = pl.BlockSpec(memory_space=pl.ANY)
    whole = pl.BlockSpec(memory_space=pltpu.VMEM)

    send, rank, mass = pl.pallas_call(
        functools.partial(pack_kernel, blocks),
        in_specs=[anywhere] * 3,
        out_shape=(
            jax.ShapeDtypeStruct((out_rows, width + part), BF16),
            jax.ShapeDtypeStruct((1, tokens), jnp.int32),
            jax.ShapeDtypeStruct((SUB, 128), F32),
        ),
        scratch_shapes=[
            pltpu.VMEM((1, tokens), jnp.int32),
            pltpu.VMEM((1, tokens), BF16),
            pltpu.VMEM((tokens, width), BF16),
            pltpu.VMEM((part // 128, out_rows, 128), F32),
            pltpu.SemaphoreType.DMA((3,)),
        ],
        compiler_params=pltpu.CompilerParams(vmem_limit_bytes=62 * 1024 * 1024),
        name="pack",
    )(routes_row, gates_row, d_out)
    recv = lax.all_to_all(send, "expert", split_axis=0, concat_axis=0, tiled=True)

    lines = [[line * RING + i for i in range(RING)] for line in range(dp // RING)]
    mass = lax.psum(mass, "dp", axis_index_groups=lines)
    mass = lax.psum(mass, "dp", axis_index_groups=[list(across) for across in zip(*lines)])

    hid = jnp.transpose(slot_hidden, (0, 2, 3, 1, 4)).reshape(slots * groups, units)
    weight = w_down.reshape(w_down.shape[1:])
    work = 2 * slots * groups * width * units
    moved = 2 * units * width
    y_out = pl.pallas_call(
        functools.partial(expert_kernel, blocks, slots),
        in_specs=[whole, anywhere],
        out_specs=whole,
        out_shape=jax.ShapeDtypeStruct((out_rows, width + part), BF16),
        scratch_shapes=[
            pltpu.VMEM((units, width), BF16),
            pltpu.VMEM((part // 128, out_rows, 128), F32),
            pltpu.SemaphoreType.DMA((2 * blocks,)),
        ],
        compiler_params=streams,
        cost_estimate=pl.CostEstimate(flops=work, bytes_accessed=moved, transcendentals=0),
        name="expert",
    )(hid, weight)
    ret = pl.pallas_call(
        functools.partial(score_kernel, width),
        out_shape=jax.ShapeDtypeStruct((out_rows, 128), F32),
        compiler_params=vmem,
        name="score",
    )(recv, y_out, mass)
    back = lax.all_to_all(ret, "expert", split_axis=0, concat_axis=0, tiled=True)
    chunk = 256
    d_hid = pl.pallas_call(
        functools.partial(hidden_kernel, blocks, slots),
        grid=(units // chunk,),
        in_specs=[
            pl.BlockSpec((out_rows, width + part), lambda i: (0, 0)),
            pl.BlockSpec((chunk, width), lambda i: (i, 0)),
            anywhere,
        ],
        out_specs=pl.BlockSpec((slots * groups, chunk), lambda i: (0, i)),
        out_shape=jax.ShapeDtypeStruct((slots * groups, units), BF16),
        scratch_shapes=[pltpu.VMEM((slots * groups, width), BF16)],
        compiler_params=streams,
        cost_estimate=pl.CostEstimate(flops=work, bytes_accessed=moved, transcendentals=0),
        name="hidden",
    )(recv, weight, ret)
    scale = experts / (routes.shape[1] * tokens * dp * groups)
    probs = pl.pallas_call(
        functools.partial(probs_kernel, blocks, scale),
        in_specs=[pl.BlockSpec(memory_space=pltpu.SMEM)] + [whole] * 4,
        out_shape=jax.ShapeDtypeStruct((experts, tokens), F32),
        compiler_params=vmem,
        name="probs",
    )(balance_coef.reshape(1, 1), routes_row, gates_row, rank, back)
    d_hidden = jnp.transpose(d_hid.reshape(1, 1, slots, groups, units), (0, 3, 1, 2, 4))
    return (probs.T, d_hidden)


def solution(mesh):
    return jax.shard_map(
        on_device,
        mesh=mesh,
        in_specs=(
            P(("dp", "expert"), None),
            P(("dp", "expert"), None),
            P(("dp", "expert"), None),
            P("dp", None, "expert", None, None),
            P("expert", None, None),
            P(),
        ),
        out_specs=(P(("dp", "expert"), None), P("dp", None, "expert", None, None)),
        check_vma=False,
    )
```

profile of v0, /device:TPU:1, one launch (start us, length us, event | category | flops | bytes accessed | tf_op | source)
XLA Modules:
  0.0 81.0 jit_solution(8515316966982362914)
XLA Ops:
  0.6 3.2 %pack.1 = (bf16[128,6400]{1,0:T(8,128)(2,1)}, s32[1,128]{1,0:T(1,128)}, f32[8,128]{1,0:T(8,128)}) custom-call(s32[1,128]{1,0:T(1,128)} %bitcast.20, bf16[1,128]{1,0:T(2,128)(2,1)} %bitcast.22, bf16[128,5120]{1,0:T(8,128)(2,1)} %rows_any.1), custom_call_target="tpu_custom_call" | custom-call | tf_op jit(solution)/shard_map/pack/pallas_call | solution.py:184
  3.8 0.0 copy-start.4
  3.8 0.0 copy-start
  3.8 17.8 %all-to-all-start = ((bf16[16,8,6400]{2,1,0:T(8,128)(2,1)}), bf16[16,8,6400]{2,1,0:T(8,128)(2,1)S(1)}, u32[]{:S(2)}, u32[]{:S(2)}) async-start(bf16[16,8,6400]{2,1,0:T(8,128)(2,1)} %bitcast.26), calls=%async_computation | async-start | bytes 3276800 | tf_op jit(solution)/shard_map/all_to_all | solution.py:202
  21.6 0.0 copy-done.4
  21.6 18.1 %psum.14 = f32[8,128]{1,0:T(8,128)S(1)} all-reduce(f32[8,128]{1,0:T(8,128)S(1)} %copy-done.4), channel_id=1, replica_groups={{0,16,32,48,64,80,96,112},{128,144,160,176,192,208,224,240},{256,272,28..., use_global_device_ids=true, to_apply=%region_0.0 | all-reduce | flops 1024 | bytes 8192 | tf_op jit(solution)/shard_map/psum | solution.py:205
  39.8 14.4 %psum.15.mass_ref = f32[8,128]{1,0:T(8,128)S(1)} all-reduce(f32[8,128]{1,0:T(8,128)S(1)} %psum.14), channel_id=1, replica_groups={{0,128,256,384,512,640,768,896},{16,144,272,400,528,656,784,912},{32,16..., use_global_device_ids=true, to_apply=%region_1.0 | all-reduce | flops 1024 | bytes 8192 | tf_op jit(solution)/shard_map/psum | solution.py:206
  54.2 0.0 copy-done
  54.2 4.5 %expert.1.y_ref = bf16[128,6400]{1,0:T(8,128)(2,1)S(1)} custom-call(bf16[160,768]{1,0:T(8,128)(2,1)S(1)} %bitcast.19, bf16[768,5120]{1,0:T(8,128)(2,1)} %bitcast.24), custom_call_target="tpu_custom_call" | custom-call | flops 1258291200 | bytes 7864320 | tf_op jit(solution)/shard_map/expert/pallas_call | solution.py:212
  58.7 2.7 %all-to-all-done = bf16[16,8,6400]{2,1,0:T(8,128)(2,1)S(1)} async-done(((bf16[16,8,6400]{2,1,0:T(8,128)(2,1)}), bf16[16,8,6400]{2,1,0:T(8,128)(2,1)S(1)}, u32[]{:S(2)}, u32[]{:S(2)}) %all-to-all-start) | async-done | bytes 1638432 | tf_op jit(solution)/shard_map/all_to_all | solution.py:202
  61.4 1.1 %score.1.after_any = f32[128,128]{1,0:T(8,128)} custom-call(bf16[128,6400]{1,0:T(8,128)(2,1)S(1)} %bitcast.16, bf16[128,6400]{1,0:T(8,128)(2,1)S(1)} %expert.1.y_ref, f32[8,128]{1,0:T(8,128)S(1)} %psum.15.mass_ref), custom_call_target="tpu_custom_call" | custom-call | tf_op jit(solution)/shard_map/score/pallas_call | solution.py:226
  62.6 9.9 %all-to-all-start.1 = ((f32[16,8,128]{2,1,0:T(8,128)}), f32[16,8,128]{2,1,0:T(8,128)S(1)}, u32[]{:S(2)}, u32[]{:S(2)}) async-start(f32[16,8,128]{2,1,0:T(8,128)} %bitcast.8), calls=%async_computation.1 | async-start | bytes 131072 | tf_op jit(solution)/shard_map/all_to_all | solution.py:232
  73.1 0.0 copy-start.1
  73.2 0.0 copy-start.2
  73.2 0.0 copy-start.3
  73.2 7.0 %hidden.1 = bf16[160,768]{1,0:T(8,128)(2,1)} custom-call(bf16[128,6400]{1,0:T(8,128)(2,1)S(1)} %bitcast.17, bf16[768,5120]{1,0:T(8,128)(2,1)} %bitcast.25, f32[128,128]{1,0:T(8,128)} %score.1.after_any), custom_call_target="tpu_custom_call" | custom-call | flops 1258291200 | bytes 7864320 | tf_op jit(solution)/shard_map/hidden/pallas_call | solution.py:234
  80.1 0.2 all-to-all-done.1
  80.3 0.0 copy-done.1
  80.3 0.0 copy-done.2
  80.3 0.0 copy-done.3
  80.3 0.7 probs.1
Async XLA Ops:
  3.8 17.8 %copy-start.4 = (f32[8,128]{1,0:T(8,128)S(1)}, f32[8,128]{1,0:T(8,128)}, u32[]{:S(2)}) copy-start(f32[8,128]{1,0:T(8,128)} %get-tuple-element.7) | copy-start | bytes 12292
  3.8 50.4 %copy-start = (bf16[1,16,1,10,768]{4,1,3,2,0:T(8,128)(2,1)S(1)}, bf16[1,16,1,10,768]{4,1,3,2,0:T(8,128)(2,1)}, u32[]{:S(2)}) copy-start(bf16[1,16,1,10,768]{4,1,3,2,0:T(8,128)(2,1)} %param.9) | copy-start | bytes 737284
  3.8 57.6 %all-to-all-start = ((bf16[16,8,6400]{2,1,0:T(8,128)(2,1)}), bf16[16,8,6400]{2,1,0:T(8,128)(2,1)S(1)}, u32[]{:S(2)}, u32[]{:S(2)}) async-start(bf16[16,8,6400]{2,1,0:T(8,128)(2,1)} %bitcast.26), calls=%async_computation | async-start | bytes 3276800 | tf_op jit(solution)/shard_map/all_to_all | solution.py:202
  62.6 17.7 %all-to-all-start.1 = ((f32[16,8,128]{2,1,0:T(8,128)}), f32[16,8,128]{2,1,0:T(8,128)S(1)}, u32[]{:S(2)}, u32[]{:S(2)}) async-start(f32[16,8,128]{2,1,0:T(8,128)} %bitcast.8), calls=%async_computation.1 | async-start | bytes 131072 | tf_op jit(solution)/shard_map/all_to_all | solution.py:232
  73.1 7.2 %copy-start.1 = (s32[128,1]{0,1:T(1,128)S(1)}, s32[128,1]{0,1:T(1,128)}, u32[]{:S(2)}) copy-start(s32[128,1]{0,1:T(1,128)} %param.7) | copy-start | bytes 1540
  73.2 7.1 %copy-start.2 = (bf16[128,1]{0,1:T(2,128)(2,1)S(1)}, bf16[128,1]{0,1:T(2,128)(2,1)}, u32[]{:S(2)}) copy-start(bf16[128,1]{0,1:T(2,128)(2,1)} %param.8) | copy-start | bytes 772
  73.2 7.1 %copy-start.3 = (s32[1,128]{1,0:T(1,128)S(1)}, s32[1,128]{1,0:T(1,128)}, u32[]{:S(2)}) copy-start(s32[1,128]{1,0:T(1,128)} %get-tuple-element.5.rank_ref) | copy-start | bytes 1540
where the time goes:
time: 81.4 us; the launch traced here: 81 us
  blocking collectives  32.6 us (40%)
  starting transfers between devices  27.7 us (34%)
  Pallas kernels  16.5 us (20%)
  waiting for transfers between devices  2.89 us (4%)
  between operations  1.35 us (2%)
    psum x1, blocking collectives, on_device(): mass = lax.psum(mass, 'dp', axis_index_groups=lines)  18.1 us
    all_to_all x1, starting transfers between devices, on_device(): lax.all_to_all(send, 'expert', split_axis=0, concat_axis=0, tiled=True)  17.8 us
    psum x1, blocking collectives, on_device(): lax.psum(mass, 'dp', axis_index_groups=[list(across) for across in zip(*l...  14.4 us
    all_to_all x1, starting transfers between devices, on_device(): lax.all_to_all(ret, 'expert', split_axis=0, concat_axis=0, tiled=True)  9.94 us
    pallas_call x1, Pallas kernels, on_device(): pl.pallas_call(functools.partial(hidden_kernel, blocks, slots), grid=(uni...  6.97 us
    pallas_call x1, Pallas kernels, on_device(): pl.pallas_call(functools.partial(expert_kernel, blocks, slots), in_specs=...  4.47 us
    pallas_call x1, Pallas kernels, on_device(): pl.pallas_call(functools.partial(pack_kernel, blocks), in_specs=[anywhere...  3.17 us
    all_to_all x1, waiting for transfers between devices, on_device(): lax.all_to_all(send, 'expert', split_axis=0, concat_axis=0, tiled=True)  2.74 us
  transfers between devices with their start and end apart: 2, of which 2 were waited for; matrix products, arithmetic and copies ran while one was open for 0% of the time, Pallas kernels for 14%

commit v1 on v0

--- a/solution.py
+++ b/solution.py
@@ -29,10 +29,13 @@
 def pack_kernel(
     blocks, routes_any, gates_any, rows_any, send_ref, rank_ref, mass_ref, routes_ref, gates_ref, rows_ref, tail_ref, sems
 ):
+    quarters = [pl.ds(i * rows_ref.shape[0] // 4, rows_ref.shape[0] // 4) for i in range(4)]
     copies = [
         pltpu.make_async_copy(routes_any, routes_ref, sems.at[0]),
         pltpu.make_async_copy(gates_any, gates_ref, sems.at[1]),
-        pltpu.make_async_copy(rows_any, rows_ref, sems.at[2]),
+    ] + [
+        pltpu.make_async_copy(rows_any.at[rows], rows_ref.at[rows], sems.at[2 + i])
+        for i, rows in enumerate(quarters)
     ]
     for copy in copies:
         copy.start()
@@ -60,7 +63,8 @@
     late = out_rows + routes * (SUB // blocks) + (rank - SUB)
     place = jnp.where(rank < SUB, routes * SUB + rank, late)
     pick = jnp.where(row == place, gates, 0.0).astype(BF16)
-    copies[2].wait()
+    for copy in copies[2:]:
+        copy.wait()
     packed = jnp.dot(pick, rows_ref[...], preferred_element_type=F32)
     send_ref[:, :width] = packed[:out_rows].astype(BF16)
     interleave(tail_ref, blocks, 0, packed[out_rows:])
@@ -194,7 +198,7 @@
             pltpu.VMEM((1, tokens), BF16),
             pltpu.VMEM((tokens, width), BF16),
             pltpu.VMEM((part // 128, out_rows, 128), F32),
-            pltpu.SemaphoreType.DMA((3,)),
+            pltpu.SemaphoreType.DMA((6,)),
         ],
         compiler_params=pltpu.CompilerParams(vmem_limit_bytes=62 * 1024 * 1024),
         name="pack",

time: 81.4 us -> 81.4 us (level)
  no operation moved by 1% of the time
where the time goes in v1:
time: 81.4 us; the launch traced here: 81 us
  blocking collectives  32.6 us (40%)
  starting transfers between devices  27.7 us (34%)
  Pallas kernels  16.4 us (20%)
  waiting for transfers between devices  2.89 us (4%)
  between operations  1.35 us (2%)
    psum x1, blocking collectives, on_device(): mass = lax.psum(mass, 'dp', axis_index_groups=lines)  18.1 us
    all_to_all x1, starting transfers between devices, on_device(): lax.all_to_all(send, 'expert', split_axis=0, concat_axis=0, tiled=True)  17.8 us
    psum x1, blocking collectives, on_device(): lax.psum(mass, 'dp', axis_index_groups=[list(across) for across in zip(*l...  14.4 us
    all_to_all x1, starting transfers between devices, on_device(): lax.all_to_all(ret, 'expert', split_axis=0, concat_axis=0, tiled=True)  9.93 us
    pallas_call x1, Pallas kernels, on_device(): pl.pallas_call(functools.partial(hidden_kernel, blocks, slots), grid=(uni...  6.97 us
    pallas_call x1, Pallas kernels, on_device(): pl.pallas_call(functools.partial(expert_kernel, blocks, slots), in_specs=...  4.47 us
    pallas_call x1, Pallas kernels, on_device(): pl.pallas_call(functools.partial(pack_kernel, blocks), in_specs=[anywhere...  3.15 us
    all_to_all x1, waiting for transfers between devices, on_device(): lax.all_to_all(send, 'expert', split_axis=0, concat_axis=0, tiled=True)  2.74 us
  transfers between devices with their start and end apart: 2, of which 2 were waited for; matrix products, arithmetic and copies ran while one was open for 0% of the time, Pallas kernels for 14%

profile of v1, /device:TPU:1, one launch (start us, length us, event | category | flops | bytes accessed | tf_op | source)
XLA Modules:
  0.0 81.0 jit_solution(4547774329788205508)
XLA Ops:
  0.6 3.1 %pack.1 = (bf16[128,6400]{1,0:T(8,128)(2,1)}, s32[1,128]{1,0:T(1,128)}, f32[8,128]{1,0:T(8,128)}) custom-call(s32[1,128]{1,0:T(1,128)} %bitcast.20, bf16[1,128]{1,0:T(2,128)(2,1)} %bitcast.22, bf16[128,5120]{1,0:T(8,128)(2,1)} %rows_any.1), custom_call_target="tpu_custom_call" | custom-call | tf_op jit(solution)/shard_map/pack/pallas_call | solution.py:188
  3.8 0.0 copy-start.4
  3.8 0.0 copy-start
  3.8 17.8 %all-to-all-start = ((bf16[16,8,6400]{2,1,0:T(8,128)(2,1)}), bf16[16,8,6400]{2,1,0:T(8,128)(2,1)S(1)}, u32[]{:S(2)}, u32[]{:S(2)}) async-start(bf16[16,8,6400]{2,1,0:T(8,128)(2,1)} %bitcast.26), calls=%async_computation | async-start | bytes 3276800 | tf_op jit(solution)/shard_map/all_to_all | solution.py:206
  21.6 0.0 copy-done.4
  21.6 18.1 %psum.14 = f32[8,128]{1,0:T(8,128)S(1)} all-reduce(f32[8,128]{1,0:T(8,128)S(1)} %copy-done.4), channel_id=1, replica_groups={{0,16,32,48,64,80,96,112},{128,144,160,176,192,208,224,240},{256,272,28..., use_global_device_ids=true, to_apply=%region_0.0 | all-reduce | flops 1024 | bytes 8192 | tf_op jit(solution)/shard_map/psum | solution.py:209
  39.7 14.4 %psum.15.mass_ref = f32[8,128]{1,0:T(8,128)S(1)} all-reduce(f32[8,128]{1,0:T(8,128)S(1)} %psum.14), channel_id=1, replica_groups={{0,128,256,384,512,640,768,896},{16,144,272,400,528,656,784,912},{32,16..., use_global_device_ids=true, to_apply=%region_1.0 | all-reduce | flops 1024 | bytes 8192 | tf_op jit(solution)/shard_map/psum | solution.py:210
  54.2 0.0 copy-done
  54.2 4.5 %expert.1.y_ref = bf16[128,6400]{1,0:T(8,128)(2,1)S(1)} custom-call(bf16[160,768]{1,0:T(8,128)(2,1)S(1)} %bitcast.19, bf16[768,5120]{1,0:T(8,128)(2,1)} %bitcast.24), custom_call_target="tpu_custom_call" | custom-call | flops 1258291200 | bytes 7864320 | tf_op jit(solution)/shard_map/expert/pallas_call | solution.py:216
  58.7 2.7 %all-to-all-done = bf16[16,8,6400]{2,1,0:T(8,128)(2,1)S(1)} async-done(((bf16[16,8,6400]{2,1,0:T(8,128)(2,1)}), bf16[16,8,6400]{2,1,0:T(8,128)(2,1)S(1)}, u32[]{:S(2)}, u32[]{:S(2)}) %all-to-all-start) | async-done | bytes 1638432 | tf_op jit(solution)/shard_map/all_to_all | solution.py:206
  61.4 1.1 %score.1.after_any = f32[128,128]{1,0:T(8,128)} custom-call(bf16[128,6400]{1,0:T(8,128)(2,1)S(1)} %bitcast.16, bf16[128,6400]{1,0:T(8,128)(2,1)S(1)} %expert.1.y_ref, f32[8,128]{1,0:T(8,128)S(1)} %psum.15.mass_ref), custom_call_target="tpu_custom_call" | custom-call | tf_op jit(solution)/shard_map/score/pallas_call | solution.py:230
  62.5 9.9 %all-to-all-start.1 = ((f32[16,8,128]{2,1,0:T(8,128)}), f32[16,8,128]{2,1,0:T(8,128)S(1)}, u32[]{:S(2)}, u32[]{:S(2)}) async-start(f32[16,8,128]{2,1,0:T(8,128)} %bitcast.8), calls=%async_computation.1 | async-start | bytes 131072 | tf_op jit(solution)/shard_map/all_to_all | solution.py:236
  73.1 0.0 copy-start.1
  73.1 0.0 copy-start.2
  73.1 0.0 copy-start.3
  73.2 7.0 %hidden.1 = bf16[160,768]{1,0:T(8,128)(2,1)} custom-call(bf16[128,6400]{1,0:T(8,128)(2,1)S(1)} %bitcast.17, bf16[768,5120]{1,0:T(8,128)(2,1)} %bitcast.25, f32[128,128]{1,0:T(8,128)} %score.1.after_any), custom_call_target="tpu_custom_call" | custom-call | flops 1258291200 | bytes 7864320 | tf_op jit(solution)/shard_map/hidden/pallas_call | solution.py:238
  80.1 0.2 all-to-all-done.1
  80.3 0.0 copy-done.1
  80.3 0.0 copy-done.2
  80.3 0.0 copy-done.3
  80.3 0.7 probs.1
Async XLA Ops:
  3.8 17.8 %copy-start.4 = (f32[8,128]{1,0:T(8,128)S(1)}, f32[8,128]{1,0:T(8,128)}, u32[]{:S(2)}) copy-start(f32[8,128]{1,0:T(8,128)} %get-tuple-element.7) | copy-start | bytes 12292
  3.8 50.4 %copy-start = (bf16[1,16,1,10,768]{4,1,3,2,0:T(8,128)(2,1)S(1)}, bf16[1,16,1,10,768]{4,1,3,2,0:T(8,128)(2,1)}, u32[]{:S(2)}) copy-start(bf16[1,16,1,10,768]{4,1,3,2,0:T(8,128)(2,1)} %param.9) | copy-start | bytes 737284
  3.8 57.6 %all-to-all-start = ((bf16[16,8,6400]{2,1,0:T(8,128)(2,1)}), bf16[16,8,6400]{2,1,0:T(8,128)(2,1)S(1)}, u32[]{:S(2)}, u32[]{:S(2)}) async-start(bf16[16,8,6400]{2,1,0:T(8,128)(2,1)} %bitcast.26), calls=%async_computation | async-start | bytes 3276800 | tf_op jit(solution)/shard_map/all_to_all | solution.py:206
  62.5 17.7 %all-to-all-start.1 = ((f32[16,8,128]{2,1,0:T(8,128)}), f32[16,8,128]{2,1,0:T(8,128)S(1)}, u32[]{:S(2)}, u32[]{:S(2)}) async-start(f32[16,8,128]{2,1,0:T(8,128)} %bitcast.8), calls=%async_computation.1 | async-start | bytes 131072 | tf_op jit(solution)/shard_map/all_to_all | solution.py:236
  73.1 7.2 %copy-start.1 = (s32[128,1]{0,1:T(1,128)S(1)}, s32[128,1]{0,1:T(1,128)}, u32[]{:S(2)}) copy-start(s32[128,1]{0,1:T(1,128)} %param.7) | copy-start | bytes 1540
  73.1 7.1 %copy-start.2 = (bf16[128,1]{0,1:T(2,128)(2,1)S(1)}, bf16[128,1]{0,1:T(2,128)(2,1)}, u32[]{:S(2)}) copy-start(bf16[128,1]{0,1:T(2,128)(2,1)} %param.8) | copy-start | bytes 772
  73.1 7.1 %copy-start.3 = (s32[1,128]{1,0:T(1,128)S(1)}, s32[1,128]{1,0:T(1,128)}, u32[]{:S(2)}) copy-start(s32[1,128]{1,0:T(1,128)} %get-tuple-element.5.rank_ref) | copy-start | bytes 1540
